TPU v7x, 128 devices: a whole 4x4x4 slice. The times are simulated.
128 devices in a mesh: row: 8 (over z_lo, x), col: 16 (over y, z_hi, core).
Axes of the slice: x: 4, y: 4, z: 4 (z_hi: 2, z_lo: 2; z = z_hi * 2 + z_lo), core: 2. Of those that a mesh axis runs over, the one named last changes fastest.
Arguments:
- patches: bfloat16 [32, 256, 384], P('row', 'col'), may hold values from -6 to 6
- in_weight: bfloat16 [384, 1536], replicated, may hold values from -0.3125 to 0.3125
- conv_weight: float32 [3, 3, 768], replicated, may hold values from -2 to 2
- proj_weight: bfloat16 [4, 768, 56], replicated, may hold values from -0.21875 to 0.21875
- step_weight: bfloat16 [4, 24, 768], replicated, may hold values from -1.25 to 1.25
- step_bias: float32 [4, 768], replicated, may hold values from -6 to -2.5
- decay_rate: float32 [4, 16, 768], replicated, as said below
- skip_gain: float32 [4, 768], replicated, may hold values from 0.5 to 1.5
- out_weight: bfloat16 [768, 384], replicated, may hold values from -0.21875 to 0.21875
Outputs:
- block_out: bfloat16 [32, 256, 384], P('row', 'col')
Inputs may be any that keep to these rules, and one draw needn't show every extreme that they name: `decay_rate`: positive rates of the state's decay per unit of step size.
All inputs are finite; a program needn't handle non-finite values.
Results may differ from a plain program's by a relative error of at most 0.0092.
Values may be sent and summed in bfloat16 or wider, within the bound.
A program may use at most 128 MiB of HBM per device.

v0:
```python
import functools

import jax
import jax.numpy as jnp
from jax import lax
from jax.experimental import pallas as pl
from jax.experimental.pallas import tpu as pltpu
from jax.sharding import PartitionSpec as P

MESH = pl.DeviceIdType.MESH
F32, BF16 = jnp.float32, jnp.bfloat16

ROWS, COLS = 8, 16
TR, TC = 4, 16
TOK = TR * TC
CH, HID = 384, 768
RANK, NS = 24, 16
KC = 8
CW = HID // KC
LANE = 128
SECOND = 64
SEG, POS = 16, 32
SPAN = SEG * POS
PEERS = 16
LOG2E = 1.4426950408889634
epsilon = 1e-05


def normalised(x):
    average = jnp.mean(x, -1, keepdims=True)
    centred = x - average
    variance = jnp.mean(centred * centred, -1, keepdims=True)
    return centred * lax.rsqrt(variance + epsilon)


def silu(v):
    return v / (1.0 + jnp.exp(-v))


def softplus(v):
    return jnp.maximum(v, 0.0) + jnp.log1p(jnp.exp(-jnp.abs(v)))


def dot(a, b):
    return jnp.dot(a, b, preferred_element_type=F32)


def lane_mask(rows):
    return lax.broadcasted_iota(jnp.int32, (rows, LANE), 1) < CW


def chunk(x, k):
    low = CW * k
    tile, off = low // LANE, low % LANE
    width = min(2 * LANE, HID - tile * LANE)
    window = x[:, tile * LANE : tile * LANE + width]
    if off:
        window = pltpu.roll(window, width - off, 1)
    return jnp.where(lane_mask(x.shape[0]), window[:, :LANE], 0.0)


def kernel(
    patches,
    in_w,
    conv_w,
    proj_w,
    step_w,
    step_b,
    decay,
    skip,
    out_w,
    out,
    halo_send,
    halo_recv,
    pad,
    gate,
    act,
    proj,
    a2a_send,
    raw,
    tokens,
    projf,
    sw,
    bias,
    dec,
    perm,
    step,
    inflow,
    hbuf,
    pbuf,
    start,
    msg,
    cbuf,
    ysum,
    ysend,
    yrecv,
    halo_ss,
    halo_rs,
    a2a_ss,
    a2a_rs,
    car_ss,
    car_rs,
    ret_ss,
    ret_rs,
):
    R = lax.axis_index("row")
    C = lax.axis_index("col")
    half = lax.rem(C, 2)
    pair = C - half + (1 - half)
    kchunk = lax.div(C, 2)

    barrier = pltpu.get_barrier_semaphore()

    def greet(r, c):
        pl.semaphore_signal(barrier, inc=1, device_id=(r, c), device_id_type=MESH)

    def row_at(o):
        return lax.rem(R + o, ROWS)

    def col_at(o):
        return lax.rem(C + o, COLS)

    for o in range(1, COLS):
        greet(R, col_at(o))
    for o in range(1, ROWS):
        greet(row_at(o), C)
        greet(row_at(o), pair)
    beside = lax.rem(C + 15 + 2 * half, COLS)
    greet(row_at(1), beside)
    greet(row_at(ROWS - 1), beside)
    pl.semaphore_wait(barrier, 15 + 7 + 7 + 2)

    x = patches[...]
    gr = lax.broadcasted_iota(jnp.int32, (32, TOK), 0)
    gt = lax.broadcasted_iota(jnp.int32, (32, TOK), 1)
    wanted = jnp.where(gr < 16, gr * TC + TC - 1, (gr - 16) * TC)
    picks = jnp.where((gt == wanted) & (lax.rem(gr, 16) < TR), 1.0, 0.0).astype(BF16)
    top, bottom = patches.at[pl.ds(0, 16)], patches.at[pl.ds(TOK - 16, 16)]
    right_edge, left_edge = halo_send.at[pl.ds(0, 16)], halo_send.at[pl.ds(16, 16)]
    rim = (
        (bottom, 1, 0),
        (top, 7, 0),
        (right_edge, 0, 1),
        (left_edge, 0, 15),
        (bottom, 1, 1),
        (bottom, 1, 15),
        (top, 7, 1),
        (top, 7, 15),
    )
    rim_copies = []
    for slot, (edge, dr, dc) in enumerate(rim):
        rim_copies.append(
            pltpu.make_async_remote_copy(
                src_ref=edge,
                dst_ref=halo_recv.at[pl.ds(slot * 16, 16)],
                send_sem=halo_ss.at[slot],
                recv_sem=halo_rs.at[slot],
                device_id=(row_at(dr), col_at(dc)),
                device_id_type=MESH,
            )
        )
    for slot in (0, 1, 4, 5, 6, 7):
        rim_copies[slot].start()
    halo_send[...] = dot(picks, x).astype(BF16)
    for slot in (2, 3):
        rim_copies[slot].start()

    normed = normalised(x.astype(F32)).astype(BF16)
    gate_in = dot(normed, in_w[:, HID:]).astype(BF16).astype(F32)
    gate_silu = silu(gate_in)
    for k in range(KC):
        gate[k] = chunk(gate_silu, k)
    own = dot(normed, in_w[:, :HID]).astype(BF16).astype(F32)
    for i in range(TR):
        pad[1 + i, 8 : 8 + TC, :] = own[i * TC : (i + 1) * TC]

    sw[...] = jnp.zeros_like(sw)
    for g in range(2):
        place = kchunk if g == 0 else R
        shift = lax.rem(HID - CW * place, HID)
        for d in range(2):
            branch = g + 2 * d

            def part(value):
                turned = pltpu.roll(value, shift, 1)[:, :LANE]
                return jnp.where(lane_mask(value.shape[0]), turned, 0.0)

            sw[g, d * SECOND : d * SECOND + RANK, d * LANE : (d + 1) * LANE] = part(
                step_w[branch].astype(F32)
            )
            bias[g, :, d * LANE : (d + 1) * LANE] = part(
                jnp.broadcast_to(step_b[branch : branch + 1, :], (8, HID))
            )
            rates = part(decay[branch]) * (-LOG2E)
            for n in range(NS):
                dec[2 * g + d, n * 8 : (n + 1) * 8, :] = jnp.broadcast_to(
                    rates[n : n + 1], (8, LANE)
                )
    po = lax.broadcasted_iota(jnp.int32, (256, 256), 0)
    pq = lax.broadcasted_iota(jnp.int32, (256, 256), 1)
    source = lax.rem(po, 8) * 32 + lax.rem(lax.div(po, 8), 2) * 16 + lax.div(po, 16)
    perm[0] = jnp.where(pq == source, 1.0, 0.0).astype(BF16)
    target = lax.rem(pq, 8) * 32 + lax.rem(lax.div(pq, 8), 2) * 16 + lax.div(pq, 16)
    perm[1] = jnp.where(po == target, 1.0, 0.0).astype(BF16)

    for slot in range(8):
        rim_copies[slot].wait_recv()
    not_first_row = jnp.where(R > 0, 1.0, 0.0)
    not_last_row = jnp.where(R < ROWS - 1, 1.0, 0.0)
    not_first_col = jnp.where(C > 0, 1.0, 0.0)
    not_last_col = jnp.where(C < COLS - 1, 1.0, 0.0)
    rim_in = dot(normalised(halo_recv[...].astype(F32)).astype(BF16), in_w[:, :HID])
    rim_in = rim_in.astype(BF16).astype(F32)
    pad[0, 8 : 8 + TC, :] = rim_in[0:16] * not_first_row
    pad[TR + 1, 8 : 8 + TC, :] = rim_in[16:32] * not_last_row
    left = rim_in[32:48] * not_first_col
    right = rim_in[48:64] * not_last_col
    for i in range(TR):
        pad[1 + i, 7:8, :] = left[i : i + 1]
        pad[1 + i, 8 + TC : 9 + TC, :] = right[i : i + 1]
    pad[0, 7:8, :] = rim_in[79:80] * (not_first_row * not_first_col)
    pad[0, 8 + TC : 9 + TC, :] = rim_in[80:81] * (not_first_row * not_last_col)
    pad[TR + 1, 7:8, :] = rim_in[111:112] * (not_last_row * not_first_col)
    pad[TR + 1, 8 + TC : 9 + TC, :] = rim_in[112:113] * (not_last_row * not_last_col)

    for i in range(TR):
        total = jnp.zeros((TC, HID), F32)
        for p in range(3):
            for q in range(3):
                total = total + pad[i + p, 7 + q : 7 + q + TC, :] * conv_w[p, q : q + 1, :]
        act[i * TC : (i + 1) * TC, :] = silu(total).astype(BF16).astype(F32)

    activated = act[...]
    low = activated.astype(BF16)
    proj[...] = jnp.zeros_like(proj)
    for branch in range(4):
        g, d = branch % 2, branch // 2
        proj[g, :, d * SECOND : d * SECOND + RANK + 2 * NS] = dot(low, proj_w[branch])
    for k in range(KC):
        part_k = chunk(activated, k).astype(BF16)
        for g in range(2):
            a2a_send[g, k, :, :LANE] = part_k
            a2a_send[g, k, :, LANE:] = proj[g].astype(BF16)

    a2a = {0: [], 1: []}
    for o in range(1, ROWS):
        peer = row_at(o)
        a2a[1].append(
            pltpu.make_async_remote_copy(
                src_ref=a2a_send.at[1, peer],
                dst_ref=tokens.at[1, pl.ds(R * TOK, TOK)],
                send_sem=a2a_ss.at[1, o],
                recv_sem=a2a_rs.at[1, o],
                device_id=(peer, C),
                device_id_type=MESH,
            )
        )
    slot = half * 8 + kchunk
    for o in range(1, COLS):
        peer = col_at(o)
        a2a[0].append(
            pltpu.make_async_remote_copy(
                src_ref=a2a_send.at[0, lax.div(peer, 2), pl.ds(lax.rem(peer, 2) * 32, 32)],
                dst_ref=raw.at[pl.ds(slot * 32, 32)],
                send_sem=a2a_ss.at[0, o],
                recv_sem=a2a_rs.at[0, o],
                device_id=(R, peer),
                device_id_type=MESH,
            )
        )
    for g in (1, 0):
        for copy in a2a[g]:
            copy.start()
    tokens[1, pl.ds(R * TOK, TOK), :] = a2a_send[1, R]
    raw[pl.ds(slot * 32, 32), :] = a2a_send[0, kchunk, pl.ds(half * 32, 32), :]

    place = (R * 2 + half, C)

    def peer_of(g, s):
        if g == 0:
            return (lax.div(s, 2), C - half + lax.rem(s, 2))
        return (R, s)

    carries = {0: [], 1: []}
    for g in range(2):
        for o in range(1, PEERS):
            s = lax.rem(place[g] + o, PEERS)
            way = jnp.where(s > place[g], 0, 1)
            carries[g].append(
                pltpu.make_async_remote_copy(
                    src_ref=msg.at[g, way],
                    dst_ref=cbuf.at[g, place[g]],
                    send_sem=car_ss.at[g, o],
                    recv_sem=car_rs.at[g, o],
                    device_id=peer_of(g, s),
                    device_id_type=MESH,
                )
            )

    def first_pass(g):
        lines = tokens[g].astype(F32)
        projf[g] = lines[:, LANE:]
        raw_step = dot(tokens[g, :, LANE:], sw[g].astype(BF16)) + bias[g, 0:1, :]
        steps = softplus(raw_step)
        for d in range(2):
            one = steps[:, d * LANE : (d + 1) * LANE]
            step[2 * g + d] = one
            inflow[2 * g + d] = one * lines[:, :LANE]
        for d in range(2):
            b = 2 * g + d
            for hf in range(2):

                def body(i, carry):
                    held, decayed = carry
                    pos = POS - 1 - i if d == 1 else i
                    row = pl.multiple_of(pos * SEG + hf * 8, 8)
                    st = step[b, pl.ds(row, 8), :]
                    fl = inflow[b, pl.ds(row, 8), :]
                    pj = projf[g, pl.ds(row, 8), :]
                    new_held, new_decayed = [], []
                    for n in range(NS):
                        a = jnp.exp2(st * dec[b, n * 8 : (n + 1) * 8, :])
                        lane = d * SECOND + RANK + n
                        w = jnp.broadcast_to(pj[:, lane : lane + 1], (8, LANE))
                        h = a * held[n] + fl * w
                        q = a * decayed[n]
                        at = pl.multiple_of((pos * NS + n) * SEG + hf * 8, 8)
                        hbuf[b, pl.ds(at, 8), :] = h
                        pbuf[b, pl.ds(at, 8), :] = q
                        new_held.append(h)
                        new_decayed.append(q)
                    return tuple(new_held), tuple(new_decayed)

                zero = jnp.zeros((8, LANE), F32)
                lax.fori_loop(
                    0,
                    POS,
                    body,
                    (tuple(zero for _ in range(NS)), tuple(zero + 1.0 for _ in range(NS))),
                )
            last = 0 if d == 1 else (POS - 1) * NS * SEG
            held = jnp.zeros((NS, LANE), F32)
            decayed = jnp.ones((NS, LANE), F32)
            for t in range(SEG):
                seg = SEG - 1 - t if d == 1 else t
                a = pbuf[b, pl.ds(last + seg, NS, stride=SEG), :]
                held = a * held + hbuf[b, pl.ds(last + seg, NS, stride=SEG), :]
                decayed = a * decayed
            msg[g, d, :NS, :] = held
            msg[g, d, NS:, :] = decayed
        for copy in carries[g]:
            copy.start()

    def second_pass(g):
        for d in range(2):
            b = 2 * g + d
            held = jnp.zeros((NS, LANE), F32)
            for t in range(PEERS):
                s = PEERS - 1 - t if d == 1 else t
                ahead = s > place[g] if d == 1 else s < place[g]
                later = cbuf[g, s, NS:, :] * held + cbuf[g, s, :NS, :]
                held = jnp.where(ahead, later, held)
            last = 0 if d == 1 else (POS - 1) * NS * SEG
            for t in range(SEG):
                seg = SEG - 1 - t if d == 1 else t
                start[b, pl.ds(seg, NS, stride=SEG), :] = held
                held = (
                    pbuf[b, pl.ds(last + seg, NS, stride=SEG), :] * held
                    + hbuf[b, pl.ds(last + seg, NS, stride=SEG), :]
                )
        for hf in range(2):

            def body(pos, carry):
                row = pl.multiple_of(pos * SEG + hf * 8, 8)
                pj = projf[g, pl.ds(row, 8), :]
                total = jnp.zeros((8, LANE), F32)
                for d in range(2):
                    b = 2 * g + d
                    for n in range(NS):
                        at = pl.multiple_of((pos * NS + n) * SEG + hf * 8, 8)
                        h = (
                            hbuf[b, pl.ds(at, 8), :]
                            + pbuf[b, pl.ds(at, 8), :] * start[b, n * SEG + hf * 8 : n * SEG + hf * 8 + 8, :]
                        )
                        lane = d * SECOND + RANK + NS + n
                        r = jnp.broadcast_to(pj[:, lane : lane + 1], (8, LANE))
                        total = total + r * h
                ysum[g, pl.ds(row, 8), :] = total
                return carry

            lax.fori_loop(0, POS, body, 0)

    for g in range(2):
        cbuf[g, place[g]] = jnp.zeros((2 * NS, LANE), F32)
    for copy in a2a[1]:
        copy.wait_recv()
    first_pass(1)
    for copy in a2a[0]:
        copy.wait_recv()
    for b in range(2):
        tokens[0, b * 256 : (b + 1) * 256, :] = dot(
            perm[0], raw[b * 256 : (b + 1) * 256, :]
        ).astype(BF16)
    first_pass(0)

    returns = {0: [], 1: []}
    for o in range(1, ROWS):
        peer = row_at(o)
        returns[1].append(
            pltpu.make_async_remote_copy(
                src_ref=ysend.at[1, pl.ds(peer * TOK, TOK)],
                dst_ref=yrecv.at[1, R],
                send_sem=ret_ss.at[1, o],
                recv_sem=ret_rs.at[1, o],
                device_id=(peer, C),
                device_id_type=MESH,
            )
        )
    for o in range(1, COLS):
        peer = col_at(o)
        at = lax.rem(peer, 2) * 8 + lax.div(peer, 2)
        returns[0].append(
            pltpu.make_async_remote_copy(
                src_ref=ysend.at[0, pl.ds(at * 32, 32)],
                dst_ref=yrecv.at[0, kchunk, pl.ds(half * 32, 32)],
                send_sem=ret_ss.at[0, o],
                recv_sem=ret_rs.at[0, o],
                device_id=(R, peer),
                device_id_type=MESH,
            )
        )

    for copy in carries[1]:
        copy.wait_recv()
    second_pass(1)
    ysend[1] = ysum[1].astype(BF16)
    for copy in returns[1]:
        copy.start()
    yrecv[1, R] = ysend[1, pl.ds(R * TOK, TOK), :]

    for copy in carries[0]:
        copy.wait_recv()
    second_pass(0)
    for b in range(2):
        ysend[0, b * 256 : (b + 1) * 256, :] = dot(
            perm[1], ysum[0, b * 256 : (b + 1) * 256, :].astype(BF16)
        ).astype(BF16)
    for copy in returns[0]:
        copy.start()
    yrecv[0, kchunk, pl.ds(half * 32, 32), :] = ysend[0, pl.ds(slot * 32, 32), :]

    gains = skip[0:1, :] + skip[1:2, :] + skip[2:3, :] + skip[3:4, :]
    skipped = act[...] * gains
    pieces = [chunk(skipped, k) for k in range(KC)]
    for g in (1, 0):
        for copy in returns[g]:
            copy.wait_recv()
    pieces = [
        pieces[k] + yrecv[0, k].astype(F32) + yrecv[1, k].astype(F32) for k in range(KC)
    ]
    average = sum(jnp.sum(z, -1, keepdims=True) for z in pieces) * (1.0 / HID)
    mask = lane_mask(TOK)
    centred = [jnp.where(mask, z - average, 0.0) for z in pieces]
    variance = sum(jnp.sum(z * z, -1, keepdims=True) for z in centred) * (1.0 / HID)
    scale = lax.rsqrt(variance + epsilon)
    result = jnp.zeros((TOK, CH), F32)
    for k in range(KC):
        gated = (centred[k] * scale * gate[k]).astype(BF16)
        result = result + dot(gated[:, :CW], out_w[k * CW : (k + 1) * CW, :])
    out[...] = result.astype(BF16)

    for copy in rim_copies:
        copy.wait_send()
    for g in range(2):
        for group in (a2a[g], carries[g], returns[g]):
            for copy in group:
                copy.wait_send()


def per_device(
    patches,
    in_weight,
    conv_weight,
    proj_weight,
    step_weight,
    step_bias,
    decay_rate,
    skip_gain,
    out_weight,
):
    vmem = pl.BlockSpec(memory_space=pltpu.VMEM)
    dma = pltpu.SemaphoreType.DMA
    result = pl.pallas_call(
        kernel,
        out_shape=jax.ShapeDtypeStruct((TOK, CH), BF16),
        in_specs=[vmem] * 9,
        out_specs=vmem,
        scratch_shapes=[
            pltpu.VMEM((32, CH), BF16),
            pltpu.VMEM((128, CH), BF16),
            pltpu.VMEM((TR + 2, 32, HID), F32),
            pltpu.VMEM((KC, TOK, LANE), F32),
            pltpu.VMEM((TOK, HID), F32),
            pltpu.VMEM((2, TOK, LANE), F32),
            pltpu.VMEM((2, KC, TOK, 2 * LANE), BF16),
            pltpu.VMEM((SPAN, 2 * LANE), BF16),
            pltpu.VMEM((2, SPAN, 2 * LANE), BF16),
            pltpu.VMEM((2, SPAN, LANE), F32),
            pltpu.VMEM((2, LANE, 2 * LANE), F32),
            pltpu.VMEM((2, 8, 2 * LANE), F32),
            pltpu.VMEM((4, NS * 8, LANE), F32),
            pltpu.VMEM((2, 256, 256), BF16),
            pltpu.VMEM((4, SPAN, LANE), F32),
            pltpu.VMEM((4, SPAN, LANE), F32),
            pltpu.VMEM((4, SPAN * NS, LANE), F32),
            pltpu.VMEM((4, SPAN * NS, LANE), F32),
            pltpu.VMEM((4, NS * SEG, LANE), F32),
            pltpu.VMEM((2, 2, 2 * NS, LANE), F32),
            pltpu.VMEM((2, PEERS, 2 * NS, LANE), F32),
            pltpu.VMEM((2, SPAN, LANE), F32),
            pltpu.VMEM((2, SPAN, LANE), BF16),
            pltpu.VMEM((2, KC, TOK, LANE), BF16),
            dma((8,)),
            dma((8,)),
            dma((2, 16)),
            dma((2, 16)),
            dma((2, 16)),
            dma((2, 16)),
            dma((2, 16)),
            dma((2, 16)),
        ],
        compiler_params=pltpu.CompilerParams(
            collective_id=0, has_side_effects=True, vmem_limit_bytes=60 * 1024 * 1024
        ),
        name="ss2d",
    )(
        patches.reshape(TOK, CH),
        in_weight,
        conv_weight,
        proj_weight,
        step_weight,
        step_bias,
        decay_rate,
        skip_gain,
        out_weight,
    )
    return result.reshape(TR, TC, CH)


def solution(mesh):
    return jax.shard_map(
        per_device,
        mesh=mesh,
        in_specs=(P("row", "col", None), P(), P(), P(), P(), P(), P(), P(), P()),
        out_specs=P("row", "col", None),
        check_vma=False,
    )
```

profile of v0, /device:TPU:1, one launch (start us, length us, event | category | flops | bytes accessed | tf_op | source)
XLA Modules:
  0.0 78.0 jit_solution(13630912583151217069)
XLA Ops:
  0.0 2.1 %copy.10.proj_w = bf16[4,768,56]{2,1,0:T(8,128)(2,1)} copy(bf16[4,768,56]{1,2,0:T(8,128)(2,1)} %param.12) | data formatting | bytes 688128 | tf_op args[3]
  2.1 74.5 %ss2d.1 = bf16[64,384]{1,0:T(8,128)(2,1)} custom-call(bf16[64,384]{1,0:T(8,128)(2,1)} %bitcast.3, bf16[384,1536]{1,0:T(8,128)(2,1)} %in_w.1, f32[3,3,768]{2,1,0:T(4,128)} %conv_w.1, bf16[4,768,56]{2,1,0:T(8,128)(2,1)} %copy.10.proj_w, bf16[4,24,768]{2,1,0:T(8,128)(2,1)} %step_w.1, f32[4,768]{1,0:T(4,128)} %step_b.1, f32[4,16,768]{2,1,0:T(8,128)} %decay.1, ...), custom_call_target="tpu_custom_call" | custom-call | tf_op jit(solution)/shard_map/ss2d/pallas_call | solution.py:493
  76.6 1.4 %copy.12 = bf16[4,16,384]{2,1,0:T(8,128)(2,1)} copy(bf16[4,16,384]{2,1,0:T(8,128)(2,1)} %bitcast.2) | data formatting | bytes 98304
where the time goes:
time: 78.2 us; the launch traced here: 78 us
  Pallas kernels  74.5 us (95%)
  local copies, waits for them, and re-layouts  3.56 us (5%)
    pallas_call x1, Pallas kernels, per_device(): pl.pallas_call(kernel, out_shape=jax.ShapeDtypeStruct((TOK, CH), BF16), i...  74.5 us
    unnamed x2, local copies, waits for them, and re-layouts  3.56 us

commit v1 on v0

--- a/solution.py
+++ b/solution.py
@@ -20,6 +20,11 @@
 LANE = 128
 SECOND = 64
 SEG, POS = 16, 32
+KIND = 3
+QUAD = KIND * LANE
+SLOT = NS // 4 * KIND
+STATE = SLOT * LANE
+MAP = 16
 SPAN = SEG * POS
 PEERS = 16
 LOG2E = 1.4426950408889634
@@ -43,6 +48,17 @@
 
 def dot(a, b):
     return jnp.dot(a, b, preferred_element_type=F32)
+
+
+def two_parts(x):
+    high = x.astype(BF16)
+    return jnp.concatenate([high, (x - high.astype(F32)).astype(BF16)], axis=1)
+
+
+def zero_one(shape, test):
+    one = lax.broadcasted_iota(jnp.int32, shape, 0)
+    other = lax.broadcasted_iota(jnp.int32, shape, 1)
+    return jnp.where(test(one, other), 1.0, 0.0).astype(BF16)
 
 
 def lane_mask(rows):
@@ -60,6 +76,16 @@
 
 
 def kernel(
+    patches_any,
+    in_w_any,
+    conv_w_any,
+    proj_w_any,
+    step_w_any,
+    step_b_any,
+    decay_any,
+    skip_any,
+    out_w_any,
+    out,
     patches,
     in_w,
     conv_w,
@@ -69,7 +95,6 @@
     decay,
     skip,
     out_w,
-    out,
     halo_send,
     halo_recv,
     pad,
@@ -79,21 +104,28 @@
     a2a_send,
     raw,
     tokens,
-    projf,
     sw,
     bias,
-    dec,
+    rates,
+    rates_wide,
     perm,
+    tile,
+    fold,
+    rep,
     step,
     inflow,
-    hbuf,
-    pbuf,
+    wide_w,
+    wide_r,
+    ends,
+    decays,
     start,
+    msg_f32,
     msg,
     cbuf,
     ysum,
     ysend,
     yrecv,
+    load_sem,
     halo_ss,
     halo_rs,
     a2a_ss,
@@ -120,21 +152,44 @@
     def col_at(o):
         return lax.rem(C + o, COLS)
 
-    for o in range(1, COLS):
-        greet(R, col_at(o))
     for o in range(1, ROWS):
         greet(row_at(o), C)
         greet(row_at(o), pair)
+    for o in range(1, COLS):
+        greet(R, col_at(o))
     beside = lax.rem(C + 15 + 2 * half, COLS)
     greet(row_at(1), beside)
     greet(row_at(ROWS - 1), beside)
+
+    loads = [
+        pltpu.make_async_copy(source, target, load_sem.at[i])
+        for i, (source, target) in enumerate(
+            (
+                (patches_any, patches),
+                (in_w_any, in_w),
+                (step_w_any, step_w),
+                (step_b_any, step_b),
+                (decay_any, decay),
+                (conv_w_any, conv_w),
+                (proj_w_any, proj_w),
+                (skip_any, skip),
+                (out_w_any, out_w),
+            )
+        )
+    ]
+    for copy in loads:
+        copy.start()
+
+    picks = zero_one(
+        (32, TOK),
+        lambda i, t: (t == jnp.where(i < 16, i * TC + TC - 1, (i - 16) * TC))
+        & (lax.rem(i, 16) < TR),
+    )
+    loads[0].wait()
+    x = patches[...]
+    halo_send[...] = dot(picks, x).astype(BF16)
     pl.semaphore_wait(barrier, 15 + 7 + 7 + 2)
 
-    x = patches[...]
-    gr = lax.broadcasted_iota(jnp.int32, (32, TOK), 0)
-    gt = lax.broadcasted_iota(jnp.int32, (32, TOK), 1)
-    wanted = jnp.where(gr < 16, gr * TC + TC - 1, (gr - 16) * TC)
-    picks = jnp.where((gt == wanted) & (lax.rem(gr, 16) < TR), 1.0, 0.0).astype(BF16)
     top, bottom = patches.at[pl.ds(0, 16)], patches.at[pl.ds(TOK - 16, 16)]
     right_edge, left_edge = halo_send.at[pl.ds(0, 16)], halo_send.at[pl.ds(16, 16)]
     rim = (
@@ -159,22 +214,41 @@
                 device_id_type=MESH,
             )
         )
-    for slot in (0, 1, 4, 5, 6, 7):
-        rim_copies[slot].start()
-    halo_send[...] = dot(picks, x).astype(BF16)
-    for slot in (2, 3):
-        rim_copies[slot].start()
-
+    for copy in rim_copies:
+        copy.start()
+
+    loads[1].wait()
     normed = normalised(x.astype(F32)).astype(BF16)
+    own = dot(normed, in_w[:, :HID]).astype(BF16).astype(F32)
+    for i in range(TR):
+        pad[1 + i, 8 : 8 + TC, :] = own[i * TC : (i + 1) * TC]
     gate_in = dot(normed, in_w[:, HID:]).astype(BF16).astype(F32)
     gate_silu = silu(gate_in)
     for k in range(KC):
         gate[k] = chunk(gate_silu, k)
-    own = dot(normed, in_w[:, :HID]).astype(BF16).astype(F32)
-    for i in range(TR):
-        pad[1 + i, 8 : 8 + TC, :] = own[i * TC : (i + 1) * TC]
-
+
+    def arrival(p):
+        return lax.rem(p, 8) * 32 + lax.rem(lax.div(p, 8), 2) * 16 + lax.div(p, 16)
+
+    perm[0] = zero_one((256, 256), lambda i, j: j == arrival(i))
+    perm[1] = zero_one((256, 256), lambda i, j: i == arrival(j))
+    tile[...] = zero_one(
+        (2 * LANE, QUAD), lambda i, j: lax.rem(i, LANE) == lax.rem(j, CW)
+    )
+    fold[...] = zero_one((QUAD, LANE), lambda i, j: lax.rem(i, CW) == j)
+    for d in range(2):
+        for i in range(2):
+            first = d * SECOND + RANK + i * NS
+            rep[2 * d + i] = zero_one(
+                (LANE, STATE), lambda k, j: k - first == lax.div(j, CW)
+            )
+
+    for copy in loads[2:5]:
+        copy.wait()
     sw[...] = jnp.zeros_like(sw)
+    quad_lane = lax.broadcasted_iota(jnp.int32, (NS, QUAD), 1)
+    quad_n = lax.broadcasted_iota(jnp.int32, (NS, QUAD), 0)
+    own_lanes = lax.div(quad_lane, CW) == lax.rem(quad_n, 4)
     for g in range(2):
         place = kchunk if g == 0 else R
         shift = lax.rem(HID - CW * place, HID)
@@ -191,18 +265,27 @@
             bias[g, :, d * LANE : (d + 1) * LANE] = part(
                 jnp.broadcast_to(step_b[branch : branch + 1, :], (8, HID))
             )
-            rates = part(decay[branch]) * (-LOG2E)
-            for n in range(NS):
-                dec[2 * g + d, n * 8 : (n + 1) * 8, :] = jnp.broadcast_to(
-                    rates[n : n + 1], (8, LANE)
-                )
-    po = lax.broadcasted_iota(jnp.int32, (256, 256), 0)
-    pq = lax.broadcasted_iota(jnp.int32, (256, 256), 1)
-    source = lax.rem(po, 8) * 32 + lax.rem(lax.div(po, 8), 2) * 16 + lax.div(po, 16)
-    perm[0] = jnp.where(pq == source, 1.0, 0.0).astype(BF16)
-    target = lax.rem(pq, 8) * 32 + lax.rem(lax.div(pq, 8), 2) * 16 + lax.div(pq, 16)
-    perm[1] = jnp.where(po == target, 1.0, 0.0).astype(BF16)
-
+            spread = dot(two_parts(part(decay[branch]) * (-LOG2E)), tile[...])
+            spread = jnp.where(own_lanes, spread, 0.0)
+            b = 2 * g + d
+            rates[b] = jnp.zeros((MAP, LANE), F32)
+            for m in range(NS // 4):
+                four = jnp.sum(spread[4 * m : 4 * m + 4], 0, keepdims=True)
+                for kind in range(KIND):
+                    j = m * KIND + kind
+                    one = four[:, kind * LANE : (kind + 1) * LANE]
+                    rates[b, j : j + 1, :] = one
+                    rates_wide[b, j * 8 : (j + 1) * 8, :] = jnp.broadcast_to(
+                        one, (8, LANE)
+                    )
+            ends[b, SLOT * SEG :, :] = jnp.zeros(((MAP - SLOT) * SEG, LANE), F32)
+            decays[b, SLOT * SEG :, :] = jnp.zeros(((MAP - SLOT) * SEG, LANE), F32)
+    place = (R * 2 + half, C)
+    for g in range(2):
+        cbuf[g, place[g]] = jnp.zeros((MAP, LANE), BF16)
+
+    loads[5].wait()
+    loads[6].wait()
     for slot in range(8):
         rim_copies[slot].wait_recv()
     not_first_row = jnp.where(R > 0, 1.0, 0.0)
@@ -235,7 +318,9 @@
     proj[...] = jnp.zeros_like(proj)
     for branch in range(4):
         g, d = branch % 2, branch // 2
-        proj[g, :, d * SECOND : d * SECOND + RANK + 2 * NS] = dot(low, proj_w[branch])
+        proj[g, :, d * SECOND : d * SECOND + RANK + 2 * NS] = lax.dot_general(
+            low, proj_w[branch], (((1,), (1,)), ((), ())), preferred_element_type=F32
+        )
     for k in range(KC):
         part_k = chunk(activated, k).astype(BF16)
         for g in range(2):
@@ -273,8 +358,6 @@
             copy.start()
     tokens[1, pl.ds(R * TOK, TOK), :] = a2a_send[1, R]
     raw[pl.ds(slot * 32, 32), :] = a2a_send[0, kchunk, pl.ds(half * 32, 32), :]
-
-    place = (R * 2 + half, C)
 
     def peer_of(g, s):
         if g == 0:
@@ -297,101 +380,118 @@
                 )
             )
 
+    def scan(b, hf, backward, with_output):
+        def body(i, carry):
+            held, sums = carry
+            pos = POS - 1 - i if backward else i
+            row = pl.multiple_of(pos * SEG + hf * 8, 8)
+            st = [step[b, pl.ds(row, 8), k * LANE : (k + 1) * LANE] for k in range(KIND)]
+            fl = [inflow[b, pl.ds(row, 8), k * LANE : (k + 1) * LANE] for k in range(KIND)]
+            new, outs = [], [None] * KIND
+            for j in range(SLOT):
+                k = j % KIND
+                lanes = slice(j * LANE, (j + 1) * LANE)
+                a = jnp.exp2(st[k] * rates_wide[b, j * 8 : (j + 1) * 8, :])
+                h = a * held[j] + fl[k] * wide_w[b, pl.ds(row, 8), lanes]
+                new.append(h)
+                if with_output:
+                    y = h * wide_r[b, pl.ds(row, 8), lanes]
+                    outs[k] = y if outs[k] is None else outs[k] + y
+            if with_output:
+                for k in range(KIND):
+                    ysum[b, pl.ds(row, 8), k * LANE : (k + 1) * LANE] = outs[k]
+                return tuple(new), sums
+            return tuple(new), tuple(sums[k] + st[k] for k in range(KIND))
+
+        zero = jnp.zeros((8, LANE), F32)
+        if with_output:
+            first = tuple(
+                start[b, j * SEG + hf * 8 : j * SEG + hf * 8 + 8, :] for j in range(SLOT)
+            )
+            lax.fori_loop(0, POS, body, (first, ()))
+            return
+        held, sums = lax.fori_loop(
+            0, POS, body, ((zero,) * SLOT, (zero,) * KIND)
+        )
+        for j in range(SLOT):
+            at = slice(j * SEG + hf * 8, j * SEG + hf * 8 + 8)
+            ends[b, at, :] = held[j]
+            decays[b, at, :] = jnp.exp2(
+                sums[j % KIND] * rates_wide[b, j * 8 : (j + 1) * 8, :]
+            )
+
+    def in_order(d, count):
+        return range(count - 1, -1, -1) if d == 1 else range(count)
+
     def first_pass(g):
-        lines = tokens[g].astype(F32)
-        projf[g] = lines[:, LANE:]
-        raw_step = dot(tokens[g, :, LANE:], sw[g].astype(BF16)) + bias[g, 0:1, :]
-        steps = softplus(raw_step)
+        packed = tokens[g, :, LANE:]
+        signal = tokens[g, :, :LANE].astype(F32)
+        steps = softplus(dot(packed, sw[g].astype(BF16)) + bias[g, 0:1, :])
         for d in range(2):
+            b = 2 * g + d
             one = steps[:, d * LANE : (d + 1) * LANE]
-            step[2 * g + d] = one
-            inflow[2 * g + d] = one * lines[:, :LANE]
+            step[b] = dot(two_parts(one), tile[...])
+            inflow[b] = dot(two_parts(one * signal), tile[...])
+            wide_w[b] = dot(packed, rep[2 * d])
+            total = jnp.sum(one, 0, keepdims=True)
+            msg_f32[g, d] = jnp.zeros((MAP, LANE), F32)
+            for i in range(3):
+                piece = total.astype(BF16).astype(F32)
+                msg_f32[g, d, SLOT + i : SLOT + i + 1, :] = piece
+                total = total - piece
         for d in range(2):
             b = 2 * g + d
             for hf in range(2):
-
-                def body(i, carry):
-                    held, decayed = carry
-                    pos = POS - 1 - i if d == 1 else i
-                    row = pl.multiple_of(pos * SEG + hf * 8, 8)
-                    st = step[b, pl.ds(row, 8), :]
-                    fl = inflow[b, pl.ds(row, 8), :]
-                    pj = projf[g, pl.ds(row, 8), :]
-                    new_held, new_decayed = [], []
-                    for n in range(NS):
-                        a = jnp.exp2(st * dec[b, n * 8 : (n + 1) * 8, :])
-                        lane = d * SECOND + RANK + n
-                        w = jnp.broadcast_to(pj[:, lane : lane + 1], (8, LANE))
-                        h = a * held[n] + fl * w
-                        q = a * decayed[n]
-                        at = pl.multiple_of((pos * NS + n) * SEG + hf * 8, 8)
-                        hbuf[b, pl.ds(at, 8), :] = h
-                        pbuf[b, pl.ds(at, 8), :] = q
-                        new_held.append(h)
-                        new_decayed.append(q)
-                    return tuple(new_held), tuple(new_decayed)
-
-                zero = jnp.zeros((8, LANE), F32)
-                lax.fori_loop(
-                    0,
-                    POS,
-                    body,
-                    (tuple(zero for _ in range(NS)), tuple(zero + 1.0 for _ in range(NS))),
+                scan(b, hf, d == 1, False)
+            held = jnp.zeros((MAP, LANE), F32)
+            for seg in in_order(d, SEG):
+                held = (
+                    decays[b, pl.ds(seg, MAP, stride=SEG), :] * held
+                    + ends[b, pl.ds(seg, MAP, stride=SEG), :]
                 )
-            last = 0 if d == 1 else (POS - 1) * NS * SEG
-            held = jnp.zeros((NS, LANE), F32)
-            decayed = jnp.ones((NS, LANE), F32)
-            for t in range(SEG):
-                seg = SEG - 1 - t if d == 1 else t
-                a = pbuf[b, pl.ds(last + seg, NS, stride=SEG), :]
-                held = a * held + hbuf[b, pl.ds(last + seg, NS, stride=SEG), :]
-                decayed = a * decayed
-            msg[g, d, :NS, :] = held
-            msg[g, d, NS:, :] = decayed
+            msg_f32[g, d, :SLOT, :] = held[:SLOT]
+            msg[g, d] = msg_f32[g, d].astype(BF16)
         for copy in carries[g]:
             copy.start()
+        for d in range(2):
+            wide_r[2 * g + d] = dot(packed, rep[2 * d + 1])
 
     def second_pass(g):
+        maps = cbuf[g].reshape(PEERS * MAP, LANE)
+        sums = dot(maps, tile[:LANE, :])
+        kind = lax.rem(lax.broadcasted_iota(jnp.int32, (MAP, LANE), 0), KIND)
+        factors = []
+        for s in range(PEERS):
+            at = s * MAP + SLOT
+            total = sums[at : at + 1] + sums[at + 1 : at + 2] + sums[at + 2 : at + 3]
+            of_slot = jnp.where(
+                kind == 0,
+                total[:, :LANE],
+                jnp.where(kind == 1, total[:, LANE : 2 * LANE], total[:, 2 * LANE :]),
+            )
+            factors.append(
+                jnp.exp2(of_slot * jnp.where(s < place[g], rates[2 * g], rates[2 * g + 1]))
+            )
         for d in range(2):
             b = 2 * g + d
-            held = jnp.zeros((NS, LANE), F32)
-            for t in range(PEERS):
-                s = PEERS - 1 - t if d == 1 else t
+            held = jnp.zeros((MAP, LANE), F32)
+            for s in in_order(d, PEERS):
                 ahead = s > place[g] if d == 1 else s < place[g]
-                later = cbuf[g, s, NS:, :] * held + cbuf[g, s, :NS, :]
+                later = factors[s] * held + cbuf[g, s].astype(F32)
                 held = jnp.where(ahead, later, held)
-            last = 0 if d == 1 else (POS - 1) * NS * SEG
-            for t in range(SEG):
-                seg = SEG - 1 - t if d == 1 else t
-                start[b, pl.ds(seg, NS, stride=SEG), :] = held
+            for seg in in_order(d, SEG):
+                start[b, pl.ds(seg, MAP, stride=SEG), :] = held
                 held = (
-                    pbuf[b, pl.ds(last + seg, NS, stride=SEG), :] * held
-                    + hbuf[b, pl.ds(last + seg, NS, stride=SEG), :]
+                    decays[b, pl.ds(seg, MAP, stride=SEG), :] * held
+                    + ends[b, pl.ds(seg, MAP, stride=SEG), :]
                 )
-        for hf in range(2):
-
-            def body(pos, carry):
-                row = pl.multiple_of(pos * SEG + hf * 8, 8)
-                pj = projf[g, pl.ds(row, 8), :]
-                total = jnp.zeros((8, LANE), F32)
-                for d in range(2):
-                    b = 2 * g + d
-                    for n in range(NS):
-                        at = pl.multiple_of((pos * NS + n) * SEG + hf * 8, 8)
-                        h = (
-                            hbuf[b, pl.ds(at, 8), :]
-                            + pbuf[b, pl.ds(at, 8), :] * start[b, n * SEG + hf * 8 : n * SEG + hf * 8 + 8, :]
-                        )
-                        lane = d * SECOND + RANK + NS + n
-                        r = jnp.broadcast_to(pj[:, lane : lane + 1], (8, LANE))
-                        total = total + r * h
-                ysum[g, pl.ds(row, 8), :] = total
-                return carry
-
-            lax.fori_loop(0, POS, body, 0)
-
-    for g in range(2):
-        cbuf[g, place[g]] = jnp.zeros((2 * NS, LANE), F32)
+            for hf in range(2):
+                scan(b, hf, d == 1, True)
+        both = ysum[2 * g] + ysum[2 * g + 1]
+        high = both.astype(BF16)
+        rest = (both - high.astype(F32)).astype(BF16)
+        return (dot(high, fold[...]) + dot(rest, fold[...])).astype(BF16)
+
     for copy in a2a[1]:
         copy.wait_recv()
     first_pass(1)
@@ -432,23 +532,24 @@
 
     for copy in carries[1]:
         copy.wait_recv()
-    second_pass(1)
-    ysend[1] = ysum[1].astype(BF16)
+    ysend[1] = second_pass(1)
     for copy in returns[1]:
         copy.start()
     yrecv[1, R] = ysend[1, pl.ds(R * TOK, TOK), :]
 
     for copy in carries[0]:
         copy.wait_recv()
-    second_pass(0)
+    rows_out = second_pass(0)
     for b in range(2):
         ysend[0, b * 256 : (b + 1) * 256, :] = dot(
-            perm[1], ysum[0, b * 256 : (b + 1) * 256, :].astype(BF16)
+            perm[1], rows_out[b * 256 : (b + 1) * 256, :]
         ).astype(BF16)
     for copy in returns[0]:
         copy.start()
     yrecv[0, kchunk, pl.ds(half * 32, 32), :] = ysend[0, pl.ds(slot * 32, 32), :]
 
+    loads[7].wait()
+    loads[8].wait()
     gains = skip[0:1, :] + skip[1:2, :] + skip[2:3, :] + skip[3:4, :]
     skipped = act[...] * gains
     pieces = [chunk(skipped, k) for k in range(KC)]
@@ -493,9 +594,18 @@
     result = pl.pallas_call(
         kernel,
         out_shape=jax.ShapeDtypeStruct((TOK, CH), BF16),
-        in_specs=[vmem] * 9,
+        in_specs=[pl.BlockSpec(memory_space=pl.ANY)] * 9,
         out_specs=vmem,
         scratch_shapes=[
+            pltpu.VMEM((TOK, CH), BF16),
+            pltpu.VMEM((CH, 2 * HID), BF16),
+            pltpu.VMEM((3, 3, HID), F32),
+            pltpu.VMEM((4, RANK + 2 * NS, HID), BF16),
+            pltpu.VMEM((4, RANK, HID), BF16),
+            pltpu.VMEM((4, HID), F32),
+            pltpu.VMEM((4, NS, HID), F32),
+            pltpu.VMEM((4, HID), F32),
+            pltpu.VMEM((HID, CH), BF16),
             pltpu.VMEM((32, CH), BF16),
             pltpu.VMEM((128, CH), BF16),
             pltpu.VMEM((TR + 2, 32, HID), F32),
@@ -505,21 +615,28 @@
             pltpu.VMEM((2, KC, TOK, 2 * LANE), BF16),
             pltpu.VMEM((SPAN, 2 * LANE), BF16),
             pltpu.VMEM((2, SPAN, 2 * LANE), BF16),
-            pltpu.VMEM((2, SPAN, LANE), F32),
             pltpu.VMEM((2, LANE, 2 * LANE), F32),
             pltpu.VMEM((2, 8, 2 * LANE), F32),
-            pltpu.VMEM((4, NS * 8, LANE), F32),
+            pltpu.VMEM((4, MAP, LANE), F32),
+            pltpu.VMEM((4, SLOT * 8, LANE), F32),
             pltpu.VMEM((2, 256, 256), BF16),
-            pltpu.VMEM((4, SPAN, LANE), F32),
-            pltpu.VMEM((4, SPAN, LANE), F32),
-            pltpu.VMEM((4, SPAN * NS, LANE), F32),
-            pltpu.VMEM((4, SPAN * NS, LANE), F32),
-            pltpu.VMEM((4, NS * SEG, LANE), F32),
-            pltpu.VMEM((2, 2, 2 * NS, LANE), F32),
-            pltpu.VMEM((2, PEERS, 2 * NS, LANE), F32),
-            pltpu.VMEM((2, SPAN, LANE), F32),
+            pltpu.VMEM((2 * LANE, QUAD), BF16),
+            pltpu.VMEM((QUAD, LANE), BF16),
+            pltpu.VMEM((4, LANE, STATE), BF16),
+            pltpu.VMEM((4, SPAN, QUAD), F32),
+            pltpu.VMEM((4, SPAN, QUAD), F32),
+            pltpu.VMEM((4, SPAN, STATE), F32),
+            pltpu.VMEM((4, SPAN, STATE), F32),
+            pltpu.VMEM((4, MAP * SEG, LANE), F32),
+            pltpu.VMEM((4, MAP * SEG, LANE), F32),
+            pltpu.VMEM((4, MAP * SEG, LANE), F32),
+            pltpu.VMEM((2, 2, MAP, LANE), F32),
+            pltpu.VMEM((2, 2, MAP, LANE), BF16),
+            pltpu.VMEM((2, PEERS, MAP, LANE), BF16),
+            pltpu.VMEM((4, SPAN, QUAD), F32),
             pltpu.VMEM((2, SPAN, LANE), BF16),
             pltpu.VMEM((2, KC, TOK, LANE), BF16),
+            dma((9,)),
             dma((8,)),
             dma((8,)),
             dma((2, 16)),
@@ -530,14 +647,14 @@
             dma((2, 16)),
         ],
         compiler_params=pltpu.CompilerParams(
-            collective_id=0, has_side_effects=True, vmem_limit_bytes=60 * 1024 * 1024
+            collective_id=0, has_side_effects=True, vmem_limit_bytes=63 * 1024 * 1024
         ),
         name="ss2d",
     )(
         patches.reshape(TOK, CH),
         in_weight,
         conv_weight,
-        proj_weight,
+        jnp.swapaxes(proj_weight, 1, 2),
         step_weight,
         step_bias,
         decay_rate,

time: 78.2 us -> 49.7 us (0.64)
  Pallas kernels: 74.5 us -> 48.1 us
  local copies, waits for them, and re-layouts: 3.56 us -> 1.42 us
    pallas_call x1, Pallas kernels: 74.5 us -> 48.1 us  [per_device(): pl.pallas_call(kernel, out_shape=jax.ShapeDtypeStruct((TOK, CH), BF16), i...]
    unnamed x2 -> x1, local copies, waits for them, and re-layouts: 3.56 us -> 1.42 us
where the time goes in v1:
time: 49.7 us; the launch traced here: 49.6 us
  Pallas kernels  48.1 us (97%)
  local copies, waits for them, and re-layouts  1.42 us (3%)
    pallas_call x1, Pallas kernels, per_device(): pl.pallas_call(kernel, out_shape=jax.ShapeDtypeStruct((TOK, CH), BF16), i...  48.1 us
    unnamed x1, local copies, waits for them, and re-layouts  1.42 us

profile of v1, /device:TPU:1, one launch (start us, length us, event | category | flops | bytes accessed | tf_op | source)
XLA Modules:
  0.0 49.6 jit_solution(7311642794515360312)
XLA Ops:
  0.0 48.1 %ss2d.1 = bf16[64,384]{1,0:T(8,128)(2,1)} custom-call(bf16[64,384]{1,0:T(8,128)(2,1)} %bitcast.5, bf16[384,1536]{1,0:T(8,128)(2,1)} %in_w_any.1, f32[3,3,768]{2,1,0:T(4,128)} %conv_w_any.1, bf16[4,56,768]{2,1,0:T(8,128)(2,1)} %bitcast.3, bf16[4,24,768]{2,1,0:T(8,128)(2,1)} %step_w_any.1, f32[4,768]{1,0:T(4,128)} %step_b_any.1, f32[4,16,768]{2,1,0:T(8,128)} %decay_any.1, ...), custom_call_target="tpu_custom_call" | custom-call | tf_op jit(solution)/shard_map/ss2d/pallas_call | solution.py:594
  48.2 1.4 %copy.11 = bf16[4,16,384]{2,1,0:T(8,128)(2,1)} copy(bf16[4,16,384]{2,1,0:T(8,128)(2,1)} %bitcast.4) | data formatting | bytes 98304

commit v2 on v1

--- a/solution.py
+++ b/solution.py
@@ -13,6 +13,7 @@
 ROWS, COLS = 8, 16
 TR, TC = 4, 16
 TOK = TR * TC
+RIM = (TR + 2) * TC
 CH, HID = 384, 768
 RANK, NS = 24, 16
 KC = 8
@@ -26,6 +27,7 @@
 STATE = SLOT * LANE
 MAP = 16
 SPAN = SEG * POS
+UNROLL = 4
 PEERS = 16
 LOG2E = 1.4426950408889634
 epsilon = 1e-05
@@ -93,11 +95,15 @@
     step_w,
     step_b,
     decay,
+    gate_w,
     skip,
     out_w,
     halo_send,
     halo_recv,
-    pad,
+    cells,
+    shift,
+    shifted,
+    normed,
     gate,
     act,
     proj,
@@ -166,12 +172,13 @@
         for i, (source, target) in enumerate(
             (
                 (patches_any, patches),
-                (in_w_any, in_w),
+                (in_w_any.at[:, pl.ds(0, HID)], in_w),
+                (conv_w_any, conv_w),
+                (proj_w_any, proj_w),
                 (step_w_any, step_w),
                 (step_b_any, step_b),
                 (decay_any, decay),
-                (conv_w_any, conv_w),
-                (proj_w_any, proj_w),
+                (in_w_any.at[:, pl.ds(HID, HID)], gate_w),
                 (skip_any, skip),
                 (out_w_any, out_w),
             )
@@ -218,14 +225,87 @@
         copy.start()
 
     loads[1].wait()
-    normed = normalised(x.astype(F32)).astype(BF16)
-    own = dot(normed, in_w[:, :HID]).astype(BF16).astype(F32)
+    normed[...] = normalised(x.astype(F32)).astype(BF16)
+    cells[:TOK, :] = dot(normed[...], in_w[...]).astype(BF16)
+    for q in range(3):
+
+        def from_cell(i, j):
+            r, c = lax.div(i, TC) - 1, lax.rem(i, TC) + (q - 1)
+            above, below, left, right = r < 0, r >= TR, c < 0, c >= TC
+            source = jnp.where(above, c, jnp.where(below, TC + c, 0)) + TOK
+            source = jnp.where(above | below, source, r * TC + c)
+            side = jnp.where(
+                above,
+                jnp.where(left, 79, 80),
+                jnp.where(below, jnp.where(left, 111, 112), jnp.where(left, 32, 48) + r),
+            )
+            source = jnp.where(left | right, side + TOK, source)
+            outside = (above & (R == 0)) | (below & (R == ROWS - 1))
+            outside = outside | (left & (C == 0)) | (right & (C == COLS - 1))
+            return (j == source) & jnp.logical_not(outside)
+
+        shift[q] = zero_one((RIM, TOK + 128), from_cell)
+
+    for slot in range(8):
+        rim_copies[slot].wait_recv()
+    cells[TOK:, :] = dot(
+        normalised(halo_recv[...].astype(F32)).astype(BF16), in_w[...]
+    ).astype(BF16)
+    for q in range(3):
+        shifted[q] = dot(shift[q], cells[...])
+    loads[2].wait()
     for i in range(TR):
-        pad[1 + i, 8 : 8 + TC, :] = own[i * TC : (i + 1) * TC]
-    gate_in = dot(normed, in_w[:, HID:]).astype(BF16).astype(F32)
-    gate_silu = silu(gate_in)
+        total = jnp.zeros((TC, HID), F32)
+        for p in range(3):
+            for q in range(3):
+                total = total + shifted[q, (i + p) * TC : (i + p + 1) * TC, :] * conv_w[p, q : q + 1, :]
+        act[i * TC : (i + 1) * TC, :] = silu(total).astype(BF16).astype(F32)
+
+    activated = act[...]
+    low = activated.astype(BF16)
+    proj[...] = jnp.zeros_like(proj)
+    loads[3].wait()
+    for branch in range(4):
+        g, d = branch % 2, branch // 2
+        proj[g, :, d * SECOND : d * SECOND + RANK + 2 * NS] = lax.dot_general(
+            low, proj_w[branch], (((1,), (1,)), ((), ())), preferred_element_type=F32
+        )
     for k in range(KC):
-        gate[k] = chunk(gate_silu, k)
+        part_k = chunk(activated, k).astype(BF16)
+        for g in range(2):
+            a2a_send[g, k, :, :LANE] = part_k
+            a2a_send[g, k, :, LANE:] = proj[g].astype(BF16)
+
+    a2a = {0: [], 1: []}
+    for o in range(1, ROWS):
+        peer = row_at(o)
+        a2a[1].append(
+            pltpu.make_async_remote_copy(
+                src_ref=a2a_send.at[1, peer],
+                dst_ref=tokens.at[1, pl.ds(R * TOK, TOK)],
+                send_sem=a2a_ss.at[1, o],
+                recv_sem=a2a_rs.at[1, o],
+                device_id=(peer, C),
+                device_id_type=MESH,
+            )
+        )
+    slot = half * 8 + kchunk
+    for o in range(1, COLS):
+        peer = col_at(o)
+        a2a[0].append(
+            pltpu.make_async_remote_copy(
+                src_ref=a2a_send.at[0, lax.div(peer, 2), pl.ds(lax.rem(peer, 2) * 32, 32)],
+                dst_ref=raw.at[pl.ds(slot * 32, 32)],
+                send_sem=a2a_ss.at[0, o],
+                recv_sem=a2a_rs.at[0, o],
+                device_id=(R, peer),
+                device_id_type=MESH,
+            )
+        )
+    for copy in a2a[1]:
+        copy.start()
+    tokens[1, pl.ds(R * TOK, TOK), :] = a2a_send[1, R]
+    raw[pl.ds(slot * 32, 32), :] = a2a_send[0, kchunk, pl.ds(half * 32, 32), :]
 
     def arrival(p):
         return lax.rem(p, 8) * 32 + lax.rem(lax.div(p, 8), 2) * 16 + lax.div(p, 16)
@@ -243,20 +323,19 @@
                 (LANE, STATE), lambda k, j: k - first == lax.div(j, CW)
             )
 
-    for copy in loads[2:5]:
+    for copy in loads[4:7]:
         copy.wait()
     sw[...] = jnp.zeros_like(sw)
     quad_lane = lax.broadcasted_iota(jnp.int32, (NS, QUAD), 1)
     quad_n = lax.broadcasted_iota(jnp.int32, (NS, QUAD), 0)
     own_lanes = lax.div(quad_lane, CW) == lax.rem(quad_n, 4)
     for g in range(2):
-        place = kchunk if g == 0 else R
-        shift = lax.rem(HID - CW * place, HID)
+        turn = lax.rem(HID - CW * (kchunk if g == 0 else R), HID)
         for d in range(2):
             branch = g + 2 * d
 
             def part(value):
-                turned = pltpu.roll(value, shift, 1)[:, :LANE]
+                turned = pltpu.roll(value, turn, 1)[:, :LANE]
                 return jnp.where(lane_mask(value.shape[0]), turned, 0.0)
 
             sw[g, d * SECOND : d * SECOND + RANK, d * LANE : (d + 1) * LANE] = part(
@@ -284,80 +363,8 @@
     for g in range(2):
         cbuf[g, place[g]] = jnp.zeros((MAP, LANE), BF16)
 
-    loads[5].wait()
-    loads[6].wait()
-    for slot in range(8):
-        rim_copies[slot].wait_recv()
-    not_first_row = jnp.where(R > 0, 1.0, 0.0)
-    not_last_row = jnp.where(R < ROWS - 1, 1.0, 0.0)
-    not_first_col = jnp.where(C > 0, 1.0, 0.0)
-    not_last_col = jnp.where(C < COLS - 1, 1.0, 0.0)
-    rim_in = dot(normalised(halo_recv[...].astype(F32)).astype(BF16), in_w[:, :HID])
-    rim_in = rim_in.astype(BF16).astype(F32)
-    pad[0, 8 : 8 + TC, :] = rim_in[0:16] * not_first_row
-    pad[TR + 1, 8 : 8 + TC, :] = rim_in[16:32] * not_last_row
-    left = rim_in[32:48] * not_first_col
-    right = rim_in[48:64] * not_last_col
-    for i in range(TR):
-        pad[1 + i, 7:8, :] = left[i : i + 1]
-        pad[1 + i, 8 + TC : 9 + TC, :] = right[i : i + 1]
-    pad[0, 7:8, :] = rim_in[79:80] * (not_first_row * not_first_col)
-    pad[0, 8 + TC : 9 + TC, :] = rim_in[80:81] * (not_first_row * not_last_col)
-    pad[TR + 1, 7:8, :] = rim_in[111:112] * (not_last_row * not_first_col)
-    pad[TR + 1, 8 + TC : 9 + TC, :] = rim_in[112:113] * (not_last_row * not_last_col)
-
-    for i in range(TR):
-        total = jnp.zeros((TC, HID), F32)
-        for p in range(3):
-            for q in range(3):
-                total = total + pad[i + p, 7 + q : 7 + q + TC, :] * conv_w[p, q : q + 1, :]
-        act[i * TC : (i + 1) * TC, :] = silu(total).astype(BF16).astype(F32)
-
-    activated = act[...]
-    low = activated.astype(BF16)
-    proj[...] = jnp.zeros_like(proj)
-    for branch in range(4):
-        g, d = branch % 2, branch // 2
-        proj[g, :, d * SECOND : d * SECOND + RANK + 2 * NS] = lax.dot_general(
-            low, proj_w[branch], (((1,), (1,)), ((), ())), preferred_element_type=F32
-        )
-    for k in range(KC):
-        part_k = chunk(activated, k).astype(BF16)
-        for g in range(2):
-            a2a_send[g, k, :, :LANE] = part_k
-            a2a_send[g, k, :, LANE:] = proj[g].astype(BF16)
-
-    a2a = {0: [], 1: []}
-    for o in range(1, ROWS):
-        peer = row_at(o)
-        a2a[1].append(
-            pltpu.make_async_remote_copy(
-                src_ref=a2a_send.at[1, peer],
-                dst_ref=tokens.at[1, pl.ds(R * TOK, TOK)],
-                send_sem=a2a_ss.at[1, o],
-                recv_sem=a2a_rs.at[1, o],
-                device_id=(peer, C),
-                device_id_type=MESH,
-            )
-        )
-    slot = half * 8 + kchunk
-    for o in range(1, COLS):
-        peer = col_at(o)
-        a2a[0].append(
-            pltpu.make_async_remote_copy(
-                src_ref=a2a_send.at[0, lax.div(peer, 2), pl.ds(lax.rem(peer, 2) * 32, 32)],
-                dst_ref=raw.at[pl.ds(slot * 32, 32)],
-                send_sem=a2a_ss.at[0, o],
-                recv_sem=a2a_rs.at[0, o],
-                device_id=(R, peer),
-                device_id_type=MESH,
-            )
-        )
-    for g in (1, 0):
-        for copy in a2a[g]:
-            copy.start()
-    tokens[1, pl.ds(R * TOK, TOK), :] = a2a_send[1, R]
-    raw[pl.ds(slot * 32, 32), :] = a2a_send[0, kchunk, pl.ds(half * 32, 32), :]
+    for copy in a2a[0]:
+        copy.start()
 
     def peer_of(g, s):
         if g == 0:
@@ -381,6 +388,8 @@
             )
 
     def scan(b, hf, backward, with_output):
+        rate = [rates_wide[b, j * 8 : (j + 1) * 8, :] for j in range(SLOT)]
+
         def body(i, carry):
             held, sums = carry
             pos = POS - 1 - i if backward else i
@@ -391,7 +400,7 @@
             for j in range(SLOT):
                 k = j % KIND
                 lanes = slice(j * LANE, (j + 1) * LANE)
-                a = jnp.exp2(st[k] * rates_wide[b, j * 8 : (j + 1) * 8, :])
+                a = jnp.exp2(st[k] * rate[j])
                 h = a * held[j] + fl[k] * wide_w[b, pl.ds(row, 8), lanes]
                 new.append(h)
                 if with_output:
@@ -408,10 +417,10 @@
             first = tuple(
                 start[b, j * SEG + hf * 8 : j * SEG + hf * 8 + 8, :] for j in range(SLOT)
             )
-            lax.fori_loop(0, POS, body, (first, ()))
+            lax.fori_loop(0, POS, body, (first, ()), unroll=UNROLL)
             return
         held, sums = lax.fori_loop(
-            0, POS, body, ((zero,) * SLOT, (zero,) * KIND)
+            0, POS, body, ((zero,) * SLOT, (zero,) * KIND), unroll=UNROLL
         )
         for j in range(SLOT):
             at = slice(j * SEG + hf * 8, j * SEG + hf * 8 + 8)
@@ -453,8 +462,6 @@
             msg[g, d] = msg_f32[g, d].astype(BF16)
         for copy in carries[g]:
             copy.start()
-        for d in range(2):
-            wide_r[2 * g + d] = dot(packed, rep[2 * d + 1])
 
     def second_pass(g):
         maps = cbuf[g].reshape(PEERS * MAP, LANE)
@@ -502,6 +509,9 @@
             perm[0], raw[b * 256 : (b + 1) * 256, :]
         ).astype(BF16)
     first_pass(0)
+    for g in (1, 0):
+        for d in range(2):
+            wide_r[2 * g + d] = dot(tokens[g, :, LANE:], rep[2 * d + 1])
 
     returns = {0: [], 1: []}
     for o in range(1, ROWS):
@@ -548,8 +558,12 @@
         copy.start()
     yrecv[0, kchunk, pl.ds(half * 32, 32), :] = ysend[0, pl.ds(slot * 32, 32), :]
 
-    loads[7].wait()
-    loads[8].wait()
+    for copy in loads[7:]:
+        copy.wait()
+    gate_in = dot(normed[...], gate_w[...]).astype(BF16).astype(F32)
+    gate_silu = silu(gate_in)
+    for k in range(KC):
+        gate[k] = chunk(gate_silu, k)
     gains = skip[0:1, :] + skip[1:2, :] + skip[2:3, :] + skip[3:4, :]
     skipped = act[...] * gains
     pieces = [chunk(skipped, k) for k in range(KC)]
@@ -559,10 +573,10 @@
     pieces = [
         pieces[k] + yrecv[0, k].astype(F32) + yrecv[1, k].astype(F32) for k in range(KC)
     ]
-    average = sum(jnp.sum(z, -1, keepdims=True) for z in pieces) * (1.0 / HID)
+    average = jnp.sum(sum(pieces), -1, keepdims=True) * (1.0 / HID)
     mask = lane_mask(TOK)
     centred = [jnp.where(mask, z - average, 0.0) for z in pieces]
-    variance = sum(jnp.sum(z * z, -1, keepdims=True) for z in centred) * (1.0 / HID)
+    variance = jnp.sum(sum(z * z for z in centred), -1, keepdims=True) * (1.0 / HID)
     scale = lax.rsqrt(variance + epsilon)
     result = jnp.zeros((TOK, CH), F32)
     for k in range(KC):
@@ -598,17 +612,21 @@
         out_specs=vmem,
         scratch_shapes=[
             pltpu.VMEM((TOK, CH), BF16),
-            pltpu.VMEM((CH, 2 * HID), BF16),
+            pltpu.VMEM((CH, HID), BF16),
             pltpu.VMEM((3, 3, HID), F32),
             pltpu.VMEM((4, RANK + 2 * NS, HID), BF16),
             pltpu.VMEM((4, RANK, HID), BF16),
             pltpu.VMEM((4, HID), F32),
             pltpu.VMEM((4, NS, HID), F32),
+            pltpu.VMEM((CH, HID), BF16),
             pltpu.VMEM((4, HID), F32),
             pltpu.VMEM((HID, CH), BF16),
             pltpu.VMEM((32, CH), BF16),
             pltpu.VMEM((128, CH), BF16),
-            pltpu.VMEM((TR + 2, 32, HID), F32),
+            pltpu.VMEM((TOK + 128, HID), BF16),
+            pltpu.VMEM((3, RIM, TOK + 128), BF16),
+            pltpu.VMEM((3, RIM, HID), F32),
+            pltpu.VMEM((TOK, CH), BF16),
             pltpu.VMEM((KC, TOK, LANE), F32),
             pltpu.VMEM((TOK, HID), F32),
             pltpu.VMEM((2, TOK, LANE), F32),
@@ -636,7 +654,7 @@
             pltpu.VMEM((4, SPAN, QUAD), F32),
             pltpu.VMEM((2, SPAN, LANE), BF16),
             pltpu.VMEM((2, KC, TOK, LANE), BF16),
-            dma((9,)),
+            dma((10,)),
             dma((8,)),
             dma((8,)),
             dma((2, 16)),

time: 49.7 us -> 45.2 us (0.909)
  Pallas kernels: 48.1 us -> 43.6 us
    pallas_call x1, Pallas kernels: 48.1 us -> 43.6 us  [per_device(): pl.pallas_call(kernel, out_shape=jax.ShapeDtypeStruct((TOK, CH), BF16), i...]
where the time goes in v2:
time: 45.2 us; the launch traced here: 45 us
  Pallas kernels  43.6 us (96%)
  local copies, waits for them, and re-layouts  1.42 us (3%)
    pallas_call x1, Pallas kernels, per_device(): pl.pallas_call(kernel, out_shape=jax.ShapeDtypeStruct((TOK, CH), BF16), i...  43.6 us
    unnamed x1, local copies, waits for them, and re-layouts  1.42 us

profile of v2, /device:TPU:1, one launch (start us, length us, event | category | flops | bytes accessed | tf_op | source)
XLA Modules:
  0.0 45.0 jit_solution(5254402233550163284)
XLA Ops:
  0.0 43.6 %ss2d.1 = bf16[64,384]{1,0:T(8,128)(2,1)} custom-call(bf16[64,384]{1,0:T(8,128)(2,1)} %bitcast.5, bf16[384,1536]{1,0:T(8,128)(2,1)} %in_w_any.1, f32[3,3,768]{2,1,0:T(4,128)} %conv_w_any.1, bf16[4,56,768]{2,1,0:T(8,128)(2,1)} %bitcast.3, bf16[4,24,768]{2,1,0:T(8,128)(2,1)} %step_w_any.1, f32[4,768]{1,0:T(4,128)} %step_b_any.1, f32[4,16,768]{2,1,0:T(8,128)} %decay_any.1, ...), custom_call_target="tpu_custom_call" | custom-call | tf_op jit(solution)/shard_map/ss2d/pallas_call | solution.py:608
  43.6 1.4 %copy.11 = bf16[4,16,384]{2,1,0:T(8,128)(2,1)} copy(bf16[4,16,384]{2,1,0:T(8,128)(2,1)} %bitcast.4) | data formatting | bytes 98304

commit v3 on v2

--- a/solution.py
+++ b/solution.py
@@ -21,13 +21,14 @@
 LANE = 128
 SECOND = 64
 SEG, POS = 16, 32
-KIND = 3
-QUAD = KIND * LANE
-SLOT = NS // 4 * KIND
-STATE = SLOT * LANE
+GROUP = 16
+KIND = CW // GROUP
+WIDE = KIND * LANE
+SLOT = 2 * KIND
+BOTH = 2 * LANE
 MAP = 16
 SPAN = SEG * POS
-UNROLL = 4
+TURN = 4
 PEERS = 16
 LOG2E = 1.4426950408889634
 epsilon = 1e-05
@@ -117,11 +118,11 @@
     perm,
     tile,
     fold,
+    gather,
     rep,
     step,
     inflow,
-    wide_w,
-    wide_r,
+    wide,
     ends,
     decays,
     start,
@@ -312,23 +313,27 @@
 
     perm[0] = zero_one((256, 256), lambda i, j: j == arrival(i))
     perm[1] = zero_one((256, 256), lambda i, j: i == arrival(j))
-    tile[...] = zero_one(
-        (2 * LANE, QUAD), lambda i, j: lax.rem(i, LANE) == lax.rem(j, CW)
-    )
-    fold[...] = zero_one((QUAD, LANE), lambda i, j: lax.rem(i, CW) == j)
+
+    def channel(j):
+        return lax.div(j, LANE) * GROUP + lax.rem(j, GROUP)
+
+    tile[...] = zero_one((2 * LANE, WIDE), lambda i, j: lax.rem(i, LANE) == channel(j))
+    fold[...] = zero_one((WIDE, LANE), lambda i, j: channel(i) == j)
+    gather[...] = zero_one((SEG, SPAN), lambda i, j: i == lax.rem(j, SEG))
     for d in range(2):
         for i in range(2):
             first = d * SECOND + RANK + i * NS
-            rep[2 * d + i] = zero_one(
-                (LANE, STATE), lambda k, j: k - first == lax.div(j, CW)
+            at = (2 * d + i) * BOTH
+            rep[:, at : at + BOTH] = zero_one(
+                (LANE, BOTH), lambda k, j: k - first == lax.div(j, GROUP)
             )
 
     for copy in loads[4:7]:
         copy.wait()
     sw[...] = jnp.zeros_like(sw)
-    quad_lane = lax.broadcasted_iota(jnp.int32, (NS, QUAD), 1)
-    quad_n = lax.broadcasted_iota(jnp.int32, (NS, QUAD), 0)
-    own_lanes = lax.div(quad_lane, CW) == lax.rem(quad_n, 4)
+    wide_lane = lax.broadcasted_iota(jnp.int32, (NS, WIDE), 1)
+    wide_n = lax.broadcasted_iota(jnp.int32, (NS, WIDE), 0)
+    own_lanes = lax.div(lax.rem(wide_lane, LANE), GROUP) == lax.rem(wide_n, 8)
     for g in range(2):
         turn = lax.rem(HID - CW * (kchunk if g == 0 else R), HID)
         for d in range(2):
@@ -348,11 +353,11 @@
             spread = jnp.where(own_lanes, spread, 0.0)
             b = 2 * g + d
             rates[b] = jnp.zeros((MAP, LANE), F32)
-            for m in range(NS // 4):
-                four = jnp.sum(spread[4 * m : 4 * m + 4], 0, keepdims=True)
+            for m in range(2):
+                eight = jnp.sum(spread[8 * m : 8 * m + 8], 0, keepdims=True)
                 for kind in range(KIND):
                     j = m * KIND + kind
-                    one = four[:, kind * LANE : (kind + 1) * LANE]
+                    one = eight[:, kind * LANE : (kind + 1) * LANE]
                     rates[b, j : j + 1, :] = one
                     rates_wide[b, j * 8 : (j + 1) * 8, :] = jnp.broadcast_to(
                         one, (8, LANE)
@@ -388,61 +393,70 @@
             )
 
     def scan(b, hf, backward, with_output):
+        g, d = b // 2, b % 2
         rate = [rates_wide[b, j * 8 : (j + 1) * 8, :] for j in range(SLOT)]
 
-        def body(i, carry):
-            held, sums = carry
-            pos = POS - 1 - i if backward else i
-            row = pl.multiple_of(pos * SEG + hf * 8, 8)
-            st = [step[b, pl.ds(row, 8), k * LANE : (k + 1) * LANE] for k in range(KIND)]
-            fl = [inflow[b, pl.ds(row, 8), k * LANE : (k + 1) * LANE] for k in range(KIND)]
-            new, outs = [], [None] * KIND
-            for j in range(SLOT):
-                k = j % KIND
-                lanes = slice(j * LANE, (j + 1) * LANE)
-                a = jnp.exp2(st[k] * rate[j])
-                h = a * held[j] + fl[k] * wide_w[b, pl.ds(row, 8), lanes]
-                new.append(h)
+        def body(i, held):
+            for u in range(TURN):
+                pos = i * TURN + u
+                pos = POS - 1 - pos if backward else pos
+                rows = pl.ds(pl.multiple_of(pos * SEG + hf * 8, 8), 8)
+
+                def part(ref, at, k):
+                    return ref[at, rows, k * LANE : (k + 1) * LANE]
+
+                st = [part(step, b, k) for k in range(KIND)]
+                fl = [part(inflow, b, k) for k in range(KIND)]
+                w = [part(wide, g, 4 * d + m) for m in range(2)]
+                r = [part(wide, g, 4 * d + 2 + m) for m in range(2)] if with_output else None
+                new, outs = [], [None] * KIND
+                for j in range(SLOT):
+                    m, k = j // KIND, j % KIND
+                    h = jnp.exp2(st[k] * rate[j]) * held[j] + fl[k] * w[m]
+                    new.append(h)
+                    if with_output:
+                        y = h * r[m]
+                        outs[k] = y if outs[k] is None else outs[k] + y
+                held = tuple(new)
                 if with_output:
-                    y = h * wide_r[b, pl.ds(row, 8), lanes]
-                    outs[k] = y if outs[k] is None else outs[k] + y
-            if with_output:
-                for k in range(KIND):
-                    ysum[b, pl.ds(row, 8), k * LANE : (k + 1) * LANE] = outs[k]
-                return tuple(new), sums
-            return tuple(new), tuple(sums[k] + st[k] for k in range(KIND))
-
-        zero = jnp.zeros((8, LANE), F32)
+                    for k in range(KIND):
+                        y = outs[k] + part(ysum, g, k) if d == 1 else outs[k]
+                        ysum[g, rows, k * LANE : (k + 1) * LANE] = y
+            return held
+
         if with_output:
             first = tuple(
                 start[b, j * SEG + hf * 8 : j * SEG + hf * 8 + 8, :] for j in range(SLOT)
             )
-            lax.fori_loop(0, POS, body, (first, ()), unroll=UNROLL)
+            lax.fori_loop(0, POS // TURN, body, first)
             return
-        held, sums = lax.fori_loop(
-            0, POS, body, ((zero,) * SLOT, (zero,) * KIND), unroll=UNROLL
-        )
+        zero = jnp.zeros((8, LANE), F32)
+        held = lax.fori_loop(0, POS // TURN, body, (zero,) * SLOT)
         for j in range(SLOT):
-            at = slice(j * SEG + hf * 8, j * SEG + hf * 8 + 8)
-            ends[b, at, :] = held[j]
-            decays[b, at, :] = jnp.exp2(
-                sums[j % KIND] * rates_wide[b, j * 8 : (j + 1) * 8, :]
-            )
+            ends[b, j * SEG + hf * 8 : j * SEG + hf * 8 + 8, :] = held[j]
 
     def in_order(d, count):
         return range(count - 1, -1, -1) if d == 1 else range(count)
 
     def first_pass(g):
         packed = tokens[g, :, LANE:]
-        signal = tokens[g, :, :LANE].astype(F32)
+        signal = dot(tokens[g, :, :LANE], tile[:LANE, :])
         steps = softplus(dot(packed, sw[g].astype(BF16)) + bias[g, 0:1, :])
+        wide[g] = dot(packed, rep[...])
         for d in range(2):
             b = 2 * g + d
-            one = steps[:, d * LANE : (d + 1) * LANE]
-            step[b] = dot(two_parts(one), tile[...])
-            inflow[b] = dot(two_parts(one * signal), tile[...])
-            wide_w[b] = dot(packed, rep[2 * d])
-            total = jnp.sum(one, 0, keepdims=True)
+            parts = two_parts(steps[:, d * LANE : (d + 1) * LANE])
+            step[b] = dot(parts, tile[...])
+            inflow[b] = step[b] * signal
+            sums = dot(gather[...], parts)
+            sums = sums[:, :LANE] + sums[:, LANE:]
+            of_lanes = dot(two_parts(sums), tile[...])
+            for j in range(SLOT):
+                k = j % KIND
+                decays[b, j * SEG : (j + 1) * SEG, :] = jnp.exp2(
+                    of_lanes[:, k * LANE : (k + 1) * LANE] * rates[b, j : j + 1, :]
+                )
+            total = jnp.sum(sums, 0, keepdims=True)
             msg_f32[g, d] = jnp.zeros((MAP, LANE), F32)
             for i in range(3):
                 piece = total.astype(BF16).astype(F32)
@@ -471,11 +485,9 @@
         for s in range(PEERS):
             at = s * MAP + SLOT
             total = sums[at : at + 1] + sums[at + 1 : at + 2] + sums[at + 2 : at + 3]
-            of_slot = jnp.where(
-                kind == 0,
-                total[:, :LANE],
-                jnp.where(kind == 1, total[:, LANE : 2 * LANE], total[:, 2 * LANE :]),
-            )
+            of_slot = total[:, :LANE]
+            for k in range(1, KIND):
+                of_slot = jnp.where(kind == k, total[:, k * LANE : (k + 1) * LANE], of_slot)
             factors.append(
                 jnp.exp2(of_slot * jnp.where(s < place[g], rates[2 * g], rates[2 * g + 1]))
             )
@@ -494,10 +506,7 @@
                 )
             for hf in range(2):
                 scan(b, hf, d == 1, True)
-        both = ysum[2 * g] + ysum[2 * g + 1]
-        high = both.astype(BF16)
-        rest = (both - high.astype(F32)).astype(BF16)
-        return (dot(high, fold[...]) + dot(rest, fold[...])).astype(BF16)
+        return dot(ysum[g].astype(BF16), fold[...]).astype(BF16)
 
     for copy in a2a[1]:
         copy.wait_recv()
@@ -509,10 +518,6 @@
             perm[0], raw[b * 256 : (b + 1) * 256, :]
         ).astype(BF16)
     first_pass(0)
-    for g in (1, 0):
-        for d in range(2):
-            wide_r[2 * g + d] = dot(tokens[g, :, LANE:], rep[2 * d + 1])
-
     returns = {0: [], 1: []}
     for o in range(1, ROWS):
         peer = row_at(o)
@@ -638,20 +643,20 @@
             pltpu.VMEM((4, MAP, LANE), F32),
             pltpu.VMEM((4, SLOT * 8, LANE), F32),
             pltpu.VMEM((2, 256, 256), BF16),
-            pltpu.VMEM((2 * LANE, QUAD), BF16),
-            pltpu.VMEM((QUAD, LANE), BF16),
-            pltpu.VMEM((4, LANE, STATE), BF16),
-            pltpu.VMEM((4, SPAN, QUAD), F32),
-            pltpu.VMEM((4, SPAN, QUAD), F32),
-            pltpu.VMEM((4, SPAN, STATE), F32),
-            pltpu.VMEM((4, SPAN, STATE), F32),
+            pltpu.VMEM((2 * LANE, WIDE), BF16),
+            pltpu.VMEM((WIDE, LANE), BF16),
+            pltpu.VMEM((SEG, SPAN), BF16),
+            pltpu.VMEM((LANE, 4 * BOTH), BF16),
+            pltpu.VMEM((4, SPAN, WIDE), F32),
+            pltpu.VMEM((4, SPAN, WIDE), F32),
+            pltpu.VMEM((2, SPAN, 4 * BOTH), F32),
             pltpu.VMEM((4, MAP * SEG, LANE), F32),
             pltpu.VMEM((4, MAP * SEG, LANE), F32),
             pltpu.VMEM((4, MAP * SEG, LANE), F32),
             pltpu.VMEM((2, 2, MAP, LANE), F32),
             pltpu.VMEM((2, 2, MAP, LANE), BF16),
             pltpu.VMEM((2, PEERS, MAP, LANE), BF16),
-            pltpu.VMEM((4, SPAN, QUAD), F32),
+            pltpu.VMEM((2, SPAN, WIDE), F32),
             pltpu.VMEM((2, SPAN, LANE), BF16),
             pltpu.VMEM((2, KC, TOK, LANE), BF16),
             dma((10,)),

time: 45.2 us -> 44.3 us (0.980)
  Pallas kernels: 43.6 us -> 42.7 us
    pallas_call x1, Pallas kernels: 43.6 us -> 42.7 us  [per_device(): pl.pallas_call(kernel, out_shape=jax.ShapeDtypeStruct((TOK, CH), BF16), i...]
where the time goes in v3:
time: 44.3 us; the launch traced here: 44.2 us
  Pallas kernels  42.7 us (96%)
  local copies, waits for them, and re-layouts  1.42 us (3%)
    pallas_call x1, Pallas kernels, per_device(): pl.pallas_call(kernel, out_shape=jax.ShapeDtypeStruct((TOK, CH), BF16), i...  42.7 us
    unnamed x1, local copies, waits for them, and re-layouts  1.42 us

profile of v3, /device:TPU:1, one launch (start us, length us, event | category | flops | bytes accessed | tf_op | source)
XLA Modules:
  0.0 44.2 jit_solution(5787951869573190091)
XLA Ops:
  0.0 42.7 %ss2d.1 = bf16[64,384]{1,0:T(8,128)(2,1)} custom-call(bf16[64,384]{1,0:T(8,128)(2,1)} %bitcast.5, bf16[384,1536]{1,0:T(8,128)(2,1)} %in_w_any.1, f32[3,3,768]{2,1,0:T(4,128)} %conv_w_any.1, bf16[4,56,768]{2,1,0:T(8,128)(2,1)} %bitcast.3, bf16[4,24,768]{2,1,0:T(8,128)(2,1)} %step_w_any.1, f32[4,768]{1,0:T(4,128)} %step_b_any.1, f32[4,16,768]{2,1,0:T(8,128)} %decay_any.1, ...), custom_call_target="tpu_custom_call" | custom-call | tf_op jit(solution)/shard_map/ss2d/pallas_call | solution.py:613
  42.8 1.4 %copy.11 = bf16[4,16,384]{2,1,0:T(8,128)(2,1)} copy(bf16[4,16,384]{2,1,0:T(8,128)(2,1)} %bitcast.4) | data formatting | bytes 98304

commit v4 on v3

--- a/solution.py
+++ b/solution.py
@@ -303,7 +303,7 @@
                 device_id_type=MESH,
             )
         )
-    for copy in a2a[1]:
+    for copy in a2a[0]:
         copy.start()
     tokens[1, pl.ds(R * TOK, TOK), :] = a2a_send[1, R]
     raw[pl.ds(slot * 32, 32), :] = a2a_send[0, kchunk, pl.ds(half * 32, 32), :]
@@ -368,7 +368,7 @@
     for g in range(2):
         cbuf[g, place[g]] = jnp.zeros((MAP, LANE), BF16)
 
-    for copy in a2a[0]:
+    for copy in a2a[1]:
         copy.start()
 
     def peer_of(g, s):
@@ -508,9 +508,6 @@
                 scan(b, hf, d == 1, True)
         return dot(ysum[g].astype(BF16), fold[...]).astype(BF16)
 
-    for copy in a2a[1]:
-        copy.wait_recv()
-    first_pass(1)
     for copy in a2a[0]:
         copy.wait_recv()
     for b in range(2):
@@ -518,6 +515,9 @@
             perm[0], raw[b * 256 : (b + 1) * 256, :]
         ).astype(BF16)
     first_pass(0)
+    for copy in a2a[1]:
+        copy.wait_recv()
+    first_pass(1)
     returns = {0: [], 1: []}
     for o in range(1, ROWS):
         peer = row_at(o)
@@ -545,13 +545,6 @@
             )
         )
 
-    for copy in carries[1]:
-        copy.wait_recv()
-    ysend[1] = second_pass(1)
-    for copy in returns[1]:
-        copy.start()
-    yrecv[1, R] = ysend[1, pl.ds(R * TOK, TOK), :]
-
     for copy in carries[0]:
         copy.wait_recv()
     rows_out = second_pass(0)
@@ -563,6 +556,13 @@
         copy.start()
     yrecv[0, kchunk, pl.ds(half * 32, 32), :] = ysend[0, pl.ds(slot * 32, 32), :]
 
+    for copy in carries[1]:
+        copy.wait_recv()
+    ysend[1] = second_pass(1)
+    for copy in returns[1]:
+        copy.start()
+    yrecv[1, R] = ysend[1, pl.ds(R * TOK, TOK), :]
+
     for copy in loads[7:]:
         copy.wait()
     gate_in = dot(normed[...], gate_w[...]).astype(BF16).astype(F32)
@@ -572,7 +572,7 @@
     gains = skip[0:1, :] + skip[1:2, :] + skip[2:3, :] + skip[3:4, :]
     skipped = act[...] * gains
     pieces = [chunk(skipped, k) for k in range(KC)]
-    for g in (1, 0):
+    for g in (0, 1):
         for copy in returns[g]:
             copy.wait_recv()
     pieces = [

time: 44.3 us -> 43.9 us (level)
  no operation moved by 1% of the time
where the time goes in v4:
time: 43.9 us; the launch traced here: 43.7 us
  Pallas kernels  42.3 us (96%)
  local copies, waits for them, and re-layouts  1.42 us (3%)
    pallas_call x1, Pallas kernels, per_device(): pl.pallas_call(kernel, out_shape=jax.ShapeDtypeStruct((TOK, CH), BF16), i...  42.3 us
    unnamed x1, local copies, waits for them, and re-layouts  1.42 us

profile of v4, /device:TPU:1, one launch (start us, length us, event | category | flops | bytes accessed | tf_op | source)
XLA Modules:
  0.0 43.7 jit_solution(8681270830618107076)
XLA Ops:
  0.0 42.3 %ss2d.1 = bf16[64,384]{1,0:T(8,128)(2,1)} custom-call(bf16[64,384]{1,0:T(8,128)(2,1)} %bitcast.5, bf16[384,1536]{1,0:T(8,128)(2,1)} %in_w_any.1, f32[3,3,768]{2,1,0:T(4,128)} %conv_w_any.1, bf16[4,56,768]{2,1,0:T(8,128)(2,1)} %bitcast.3, bf16[4,24,768]{2,1,0:T(8,128)(2,1)} %step_w_any.1, f32[4,768]{1,0:T(4,128)} %step_b_any.1, f32[4,16,768]{2,1,0:T(8,128)} %decay_any.1, ...), custom_call_target="tpu_custom_call" | custom-call | tf_op jit(solution)/shard_map/ss2d/pallas_call | solution.py:613
  42.3 1.4 %copy.11 = bf16[4,16,384]{2,1,0:T(8,128)(2,1)} copy(bf16[4,16,384]{2,1,0:T(8,128)(2,1)} %bitcast.4) | data formatting | bytes 98304
